TPU v7x, 128 devices: a whole 4x4x4 slice. The times are simulated.
128 devices in a mesh: row: 8 (over z_hi, x), col: 16 (over y, z_lo, core).
Axes of the slice: x: 4, y: 4, z: 4 (z_hi: 2, z_lo: 2; z = z_hi * 2 + z_lo), core: 2. Of those that a mesh axis runs over, the one named last changes fastest.
Arguments:
- position: float32 [3, 65536], P(None, ('row', 'col')), may hold values from 0 to 1
- normal: float32 [3, 65536], P(None, ('row', 'col')), may hold values from -1 to 1, as said below
- area: float32 [65536], P(('row', 'col')), may hold values from 0.00061035156 to 0.0061035156
- emission: float32 [32, 65536], P(None, ('row', 'col')), may hold values from 0.05 to 1
- reflect: float32 [32, 65536], P(None, ('row', 'col')), may hold values from 0.3 to 0.95
- pair_list: int32 [8, 16, 128], P('row', 'col'), may hold values from 0 to 511, as said below
- pair_count: int32 [8, 16], P('row', 'col'), may hold values from 32 to 128
- visible: int32 [8, 16, 128, 32, 256], P('row', 'col'), may hold values from 0 to 255
Outputs:
- radiosity: float32 [32, 65536], P(None, ('row', 'col'))
Inputs may be any that keep to these rules, and one draw needn't show every extreme that they name: `pair_list`: the 128 codes of one device are distinct. `normal`: unit vectors.
All inputs are finite; a program needn't handle non-finite values.
Results may differ from a plain program's by a relative error of at most 0.0003.
Values sent between devices are 32-bit elements; how exact they have to be, the bound alone decides.
A program may use at most 128 MiB of HBM per device.

v0:
```python
import math

import jax
import jax.numpy as jnp
from jax import lax
from jax.sharding import PartitionSpec as P

ITERS = 3


def tile_factor(receiver_pos, receiver_nrm, source_pos, source_nrm, source_area, packed_bits):
    shifts = jnp.arange(8, dtype=jnp.int32)
    unpacked = jnp.bitwise_and(jnp.right_shift(packed_bits[:, None, :], shifts[None, :, None]), 1)
    seen_mask = unpacked.reshape(-1, packed_bits.shape[1]).astype(jnp.float32)
    offset_vec = source_pos[:, :, None] - receiver_pos[:, None, :]
    receiver_cos = jnp.maximum(jnp.sum(receiver_nrm[:, None, :] * offset_vec, axis=0), 0.0)
    source_cos = jnp.maximum(-jnp.sum(source_nrm[:, :, None] * offset_vec, axis=0), 0.0)
    spread = jnp.sum(offset_vec * offset_vec, axis=0) + source_area[:, None] / math.pi
    return (
        seen_mask * receiver_cos * source_cos * source_area[:, None] / (math.pi * spread * spread)
    )


def body(position, normal, area, emission, reflect, pair_list, pair_count, visible):
    piece_len = position.shape[1]
    block_len = visible.shape[-1]
    word_count = visible.shape[-2]
    band_count = emission.shape[0]
    receiver_pos, receiver_nrm = (
        lax.all_gather(position, "col", axis=1, tiled=True),
        lax.all_gather(normal, "col", axis=1, tiled=True),
    )
    source_pos, source_nrm, source_rows = (
        lax.all_gather(position, "row", axis=1, tiled=True),
        lax.all_gather(normal, "row", axis=1, tiled=True),
        lax.all_gather(area[None, :], "row", axis=1, tiled=True),
    )
    source_area = source_rows[0]
    source_blocks = source_pos.shape[1] // block_len
    receiver_blocks = receiver_pos.shape[1] // block_len
    pair_codes = pair_list.reshape(-1)
    slot_total = pair_codes.shape[0]
    live_count = pair_count.reshape(())
    packed_all = visible.reshape(-1, word_count, block_len)
    receiver_ids = pair_codes // source_blocks
    source_ids = pair_codes % source_blocks

    def build_tile(item):
        rec_id, src_id, packed_bits = item
        rec_start = rec_id * block_len
        src_start = src_id * block_len
        return tile_factor(
            lax.dynamic_slice_in_dim(receiver_pos, rec_start, block_len, 1),
            lax.dynamic_slice_in_dim(receiver_nrm, rec_start, block_len, 1),
            lax.dynamic_slice_in_dim(source_pos, src_start, block_len, 1),
            lax.dynamic_slice_in_dim(source_nrm, src_start, block_len, 1),
            lax.dynamic_slice_in_dim(source_area, src_start, block_len, 0),
            packed_bits,
        )

    factors = lax.map(build_tile, (receiver_ids, source_ids, packed_all))
    live_flags = (jnp.arange(slot_total, dtype=jnp.int32) < live_count).astype(jnp.float32)
    placement = (
        receiver_ids[:, None] == jnp.arange(receiver_blocks, dtype=jnp.int32)[None, :]
    ).astype(jnp.float32) * live_flags[:, None]
    radiosity = emission
    for sweep_index in range(ITERS):
        outgoing = lax.all_gather(radiosity, "row", axis=1, tiled=True)
        source_slices = jnp.take(
            outgoing.reshape(band_count, source_blocks, block_len), source_ids, axis=1
        )
        contribs = jnp.einsum(
            "bsa,sak->sbk",
            source_slices,
            factors,
            precision=lax.Precision.HIGHEST,
            preferred_element_type=jnp.float32,
        )
        placed = jnp.einsum(
            "sbk,sg->bgk",
            contribs,
            placement,
            precision=lax.Precision.HIGHEST,
            preferred_element_type=jnp.float32,
        )
        partial_sum = placed.reshape(band_count, receiver_blocks * block_len)
        summed = lax.psum(partial_sum, "col")
        own_share = lax.dynamic_slice_in_dim(
            summed, lax.axis_index("col") * piece_len, piece_len, 1
        )
        radiosity = emission + reflect * own_share
    return radiosity


def solution(mesh):
    placed = (
        P(None, ("row", "col")),
        P(None, ("row", "col")),
        P(("row", "col")),
        P(None, ("row", "col")),
        P(None, ("row", "col")),
        P("row", "col", None),
        P("row", "col"),
        P("row", "col", None, None, None),
    )
    return jax.shard_map(
        body, mesh=mesh, in_specs=placed, out_specs=P(None, ("row", "col")), check_vma=False
    )
```

profile of v0, /device:TPU:1, one launch (start us, length us, event | category | flops | bytes accessed | tf_op | source)
XLA Modules:
  0.0 1341.0 jit_solution(5586130605823531881)
XLA Ops:
  7.9 22.2 %all_gather.27 = f32[3,8192]{1,0:T(4,128)S(1)} all-gather(f32[3,512]{1,0:T(4,128)} %param.12), channel_id=1, replica_groups=mesh['row'=8,'col'=16] {'col'}, dimensions={1}, use_global_device_ids=true | all-gather | bytes 104448 | tf_op jit(solution)/shard_map/all_gather | solution.py:30
  30.1 29.3 %all_gather.26 = f32[3,4096]{1,0:T(4,128)S(1)} all-gather(f32[3,512]{1,0:T(4,128)} %param.12), channel_id=1, replica_groups=mesh['row'=8,'col'=16] {'row'}, dimensions={1}, use_global_device_ids=true | all-gather | bytes 55296 | tf_op jit(solution)/shard_map/all_gather | solution.py:34
  59.4 22.6 %all_gather.25 = f32[3,8192]{1,0:T(4,128)S(1)} all-gather(f32[3,512]{1,0:T(4,128)} %param.13), channel_id=1, replica_groups=mesh['row'=8,'col'=16] {'col'}, dimensions={1}, use_global_device_ids=true | all-gather | bytes 104448 | tf_op jit(solution)/shard_map/all_gather | solution.py:31
  82.0 28.3 %all_gather.28 = f32[3,4096]{1,0:T(4,128)S(1)} all-gather(f32[3,512]{1,0:T(4,128)} %param.13), channel_id=1, replica_groups=mesh['row'=8,'col'=16] {'row'}, dimensions={1}, use_global_device_ids=true | all-gather | bytes 55296 | tf_op jit(solution)/shard_map/all_gather | solution.py:35
  110.3 25.2 %all-gather.1 = f32[8,1,512]{2,1,0:T(1,128)S(1)} all-gather(f32[1,1,512]{2,1,0:T(1,128)} %bitcast.115), channel_id=2, replica_groups=mesh['row'=8,'col'=16] {'row'}, dimensions={0}, use_global_device_ids=true | all-gather | bytes 18432 | tf_op jit(solution)/shard_map/all_gather | solution.py:36
  135.5 616.9 %while.10 = (s32[]{:T(128)}, f32[128,256,256]{2,1,0:T(8,128)}, s32[128,32,256]{2,1,0:T(8,128)}, s32[128]{0:T(128)S(1)}, f32[3,8192]{1,0:T(4,128)S(1)}, /*index=5...) while((s32[]{:T(128)}, f32[128,256,256]{2,1,0:T(8,128)}, ...), condition=%wide.region_4.6_spmd, body=%wide.region_0.5_spmd.sunk | while | flops 2031882 | bytes 1980185 | solution.py:61
  158.7 0.9 fusion.56
  163.5 0.9 fusion.56
  178.0 0.9 fusion.56
  192.5 0.9 fusion.56
  197.3 0.9 fusion.56
  231.0 0.9 fusion.56
  240.7 0.9 fusion.56
  303.3 0.9 fusion.56
  308.2 0.9 fusion.56
  317.8 0.9 fusion.56
  332.3 0.9 fusion.56
  380.5 0.9 fusion.56
  467.2 0.9 fusion.56
  472.0 0.9 fusion.56
  505.8 0.9 fusion.56
  539.5 0.9 fusion.56
  549.1 0.9 fusion.56
  578.1 0.9 fusion.56
  611.8 0.9 fusion.56
  616.6 0.9 fusion.56
  640.8 0.9 fusion.56
  689.0 0.9 fusion.56
  727.5 0.9 fusion.56
  752.5 28.5 %all_gather.24 = f32[32,4096]{1,0:T(8,128)S(1)} all-gather(f32[32,512]{1,0:T(8,128)S(1)} %copy-done), channel_id=1, replica_groups=mesh['row'=8,'col'=16] {'row'}, dimensions={1}, use_global_device_ids=true | all-gather | bytes 589824 | tf_op jit(solution)/shard_map/all_gather | solution.py:68
  781.7 2.9 gather_fusion
  784.5 25.0 %fusion.12 = f32[128,32,256]{2,1,0:T(8,128)} fusion(f32[128,256,256]{2,1,0:T(8,128)} %get-tuple-element.58, f32[128,32,256]{2,1,0:T(8,128)} %gather_fusion, pred[128]{0:T(512)(128)(4,1)S(1)} %get-tuple-element.84), kind=kOutput, calls=%fused_computation.29 | convolution fusion | flops 3222274048 | bytes 41943168 | tf_op jit(solution)/shard_map/bsa,sak->sbk/dot_general | solution.py:72
  809.5 7.0 fusion.18
  816.5 1.6 copy.30
  818.2 133.0 %all-reduce.4.cloned.1.call-done = f32[32,8192]{1,0:T(8,128)} async-done(((f32[32,8192]{1,0:T(8,128)}), f32[32,8192]{1,0:T(8,128)}) %all-reduce.4.cloned.1.call-update) | async-done | bytes 1048592 | tf_op jit(solution)/shard_map/psum | solution.py:87
  952.1 29.6 %all_gather.30 = f32[32,4096]{1,0:T(8,128)S(1)} all-gather(f32[32,512]{1,0:T(8,128)S(1)} %multiply_add_fusion.2), channel_id=1, replica_groups=mesh['row'=8,'col'=16] {'row'}, dimensions={1}, use_global_device_ids=true | all-gather | bytes 589824 | tf_op jit(solution)/shard_map/all_gather | solution.py:68
  981.7 2.9 gather_fusion.1
  984.6 25.0 %fusion.10 = f32[128,32,256]{2,1,0:T(8,128)} fusion(f32[128,256,256]{2,1,0:T(8,128)} %get-tuple-element.58, f32[128,32,256]{2,1,0:T(8,128)} %gather_fusion.1, pred[128]{0:T(512)(128)(4,1)S(1)} %get-tuple-element.84), kind=kOutput, calls=%fused_computation.27 | convolution fusion | flops 3222274048 | bytes 41943168 | tf_op jit(solution)/shard_map/bsa,sak->sbk/dot_general | solution.py:72
  1009.6 6.9 fusion.16
  1016.5 1.6 copy.31
  1018.2 123.9 %all-reduce.6.cloned.1.call-done = f32[32,8192]{1,0:T(8,128)} async-done(((f32[32,8192]{1,0:T(8,128)}), f32[32,8192]{1,0:T(8,128)}) %all-reduce.6.cloned.1.call-update) | async-done | bytes 1048592 | tf_op jit(solution)/shard_map/psum | solution.py:87
  1142.9 29.6 %all_gather.31 = f32[32,4096]{1,0:T(8,128)S(1)} all-gather(f32[32,512]{1,0:T(8,128)S(1)} %multiply_add_fusion.1), channel_id=1, replica_groups=mesh['row'=8,'col'=16] {'row'}, dimensions={1}, use_global_device_ids=true | all-gather | bytes 589824 | tf_op jit(solution)/shard_map/all_gather | solution.py:68
  1172.6 2.9 gather_fusion.2
  1175.5 25.0 %fusion.8 = f32[128,32,256]{2,1,0:T(8,128)} fusion(f32[128,256,256]{2,1,0:T(8,128)} %get-tuple-element.58, f32[128,32,256]{2,1,0:T(8,128)} %gather_fusion.2, pred[128]{0:T(512)(128)(4,1)S(1)} %get-tuple-element.84), kind=kOutput, calls=%fused_computation.25 | convolution fusion | flops 3222274048 | bytes 41943168 | tf_op jit(solution)/shard_map/bsa,sak->sbk/dot_general | solution.py:72
  1200.5 6.9 fusion.14
  1207.4 1.6 copy.32
  1209.1 123.9 %all-reduce.8.cloned.1.call-done = f32[32,8192]{1,0:T(8,128)} async-done(((f32[32,8192]{1,0:T(8,128)}), f32[32,8192]{1,0:T(8,128)}) %all-reduce.8.cloned.1.call-update) | async-done | bytes 1048592 | tf_op jit(solution)/shard_map/psum | solution.py:87
  1333.0 1.5 multiply_add_fusion
  (1278 shorter events, 421.0 us)
Async XLA Ops:
  6.5 944.7 %all-reduce.4.cloned.1.call-start = ((), (), s32[]{:S(2)}) async-start(), calls=%async_computation | async-start | bytes 2097152 | tf_op jit(solution)/shard_map/psum | solution.py:87
  135.5 617.0 %copy-start = (f32[32,512]{1,0:T(8,128)S(1)}, f32[32,512]{1,0:T(8,128)}, u32[]{:S(2)}) copy-start(f32[32,512]{1,0:T(8,128)} %param.15) | copy-start | bytes 196612
  809.5 141.7 %copy-start.1 = (f32[32,512]{1,0:T(8,128)S(1)}, f32[32,512]{1,0:T(8,128)}, u32[]{:S(2)}) copy-start(f32[32,512]{1,0:T(8,128)} %param.16) | copy-start | bytes 196612
  818.2 323.9 %all-reduce.6.cloned.1.call-start = ((), (), s32[]{:S(2)}) async-start(), calls=%async_computation.1 | async-start | bytes 2097152 | tf_op jit(solution)/shard_map/psum | solution.py:87
  1018.2 314.8 %all-reduce.8.cloned.1.call-start = ((), (), s32[]{:S(2)}) async-start(), calls=%async_computation.2 | async-start | bytes 2097152 | tf_op jit(solution)/shard_map/psum | solution.py:87
Sparse Core Ops, SparseCore 0:
  818.3 132.8 all-reduce.3
  1018.3 123.7 all-reduce.5
  1209.2 123.7 all-reduce.7
where the time goes:
time: 1350 us; the launch traced here: 1340 us
  waiting for transfers between devices  381 us (28%)
  local copies, waits for them, and re-layouts  292 us (22%)
  blocking collectives  215 us (16%)
  loops' own time  178 us (13%)
  other arithmetic  165 us (12%)
  matrix products  95.8 us (7%)
  between operations  13.8 us (1%)
    psum x3, waiting for transfers between devices, body(): summed = lax.psum(partial_sum, 'col')  381 us
    another operation x1, loops' own time, body(): factors = lax.map(build_tile, (receiver_ids, source_ids, packed_all))  178 us
    dynamic_slice x256, local copies, waits for them, and re-layouts, body(): factors = lax.map(build_tile, (receiver_ids, source_ids, packed_all))  166 us
    dynamic_update_slice x128, other arithmetic, body(): factors = lax.map(build_tile, (receiver_ids, source_ids, packed_all))  115 us
    shift_right_arithmetic x384, local copies, waits for them, and re-layouts, tile_factor(): jnp.right_shift(packed_bits[:, None, :], shifts[None, :, None])  109 us
    all_gather x3, blocking collectives, body(): outgoing = lax.all_gather(radiosity, 'row', axis=1, tiled=True)  87.7 us
    dot_general x3, matrix products, body(): jnp.einsum('bsa,sak->sbk', source_slices, factors, precision=lax.Precisio...  75 us
    reduce_sum x128, other arithmetic, tile_factor(): jnp.sum(receiver_nrm[:, None, :] * offset_vec, axis=0)  34.6 us
  transfers between devices with their start and end apart: 3, of which 3 were waited for; matrix products, arithmetic and copies ran while one was open for 0% of the time, Pallas kernels for 0%

commit v1 on v0

v1 whole, which is shorter than its diff:
```python
import functools
import math

import jax
import jax.numpy as jnp
from jax import lax
from jax.experimental import pallas as pl
from jax.experimental.pallas import tpu as pltpu
from jax.sharding import PartitionSpec as P

ITERS = 3
MESH = pl.DeviceIdType.MESH
F32, BF16, I32 = jnp.float32, jnp.bfloat16, jnp.int32
CHUNK = 64
SLOT_STEP = 4
SWEEP_STEP = 8


def pieces(x):
    high = x.astype(BF16).astype(F32)
    rest = x - high
    middle = rest.astype(BF16).astype(F32)
    return high, middle, rest - middle


def kernel(
    n_row, n_col, ints, floats, position, normal, area, emission, reflect, visible, out,
    factor_hi, factor_lo, seen_words, running, lhs, rhs, shuffle, turned, own_source, own_receiver,
    own_sent, source_rows, receiver_rows, gathered, outgoing, pair_out, pair_in, mine, peer_in,
    vis_sem, src_send, src_recv, rec_send, rec_recv, out_send, out_recv, pair_send, pair_recv, peer_send, peer_recv,
):
    slots, words, block = visible.shape
    bands, piece = emission.shape
    per_piece = piece // block
    n_chip = n_col // 2
    n_source = per_piece * n_row
    row, col = lax.axis_index("row"), lax.axis_index("col")
    chip, core = col // 2, col % 2

    fetch = pltpu.make_async_copy(visible, seen_words, vis_sem)
    fetch.start()

    centre = position[...] - 0.5
    facing = normal[...]
    weight = area[...] * (1.0 / math.pi)
    along = jnp.sum(facing * centre, axis=0, keepdims=True)
    square = jnp.sum(centre * centre, axis=0, keepdims=True)
    own_source[0:3, :] = centre
    own_source[3:4, :] = square + weight
    own_source[4:7, :] = facing * weight
    own_source[7:8, :] = -along * weight
    own_receiver[0:3, :] = facing
    own_receiver[3:4, :] = -along
    own_receiver[4:7, :] = centre
    own_receiver[7:8, :] = square

    here = lax.broadcasted_iota(I32, (block, block), 0)
    there = lax.broadcasted_iota(I32, (block, block), 1)
    shuffle[...] = jnp.where(here == (there % words) * 8 + there // words, 1.0, 0.0).astype(BF16)

    def shuffled(x, part):
        cut = x[:, part * block : (part + 1) * block]
        stacked = jnp.concatenate([v.astype(BF16) for v in pieces(cut)], axis=0)
        moved = jnp.dot(stacked, shuffle[...], preferred_element_type=F32)
        return moved[:bands] + moved[bands : 2 * bands] + moved[2 * bands :]

    def set_sent(sweep, x):
        for part in range(per_piece):
            own_sent[sweep, :, part * block : (part + 1) * block] = shuffled(x, part)

    set_sent(0, emission[...])

    barrier = pltpu.get_barrier_semaphore()
    for k in range(1, n_row):
        pl.semaphore_signal(barrier, inc=1, device_id=((row + k) % n_row, col), device_id_type=MESH)
    for k in range(1, n_col):
        pl.semaphore_signal(barrier, inc=1, device_id=(row, (col + k) % n_col), device_id_type=MESH)
    pl.semaphore_wait(barrier, n_row + n_col - 2)

    def to_source(k):
        return pltpu.make_async_remote_copy(
            own_source, source_rows.at[k], src_send.at[k], src_recv.at[k],
            device_id=((row + k) % n_row, col), device_id_type=MESH)

    def to_receiver(k):
        return pltpu.make_async_remote_copy(
            own_receiver, receiver_rows.at[k], rec_send.at[k], rec_recv.at[k],
            device_id=(row, (col + k) % n_col), device_id_type=MESH)

    def to_row(sweep, k):
        return pltpu.make_async_remote_copy(
            own_sent.at[sweep], gathered.at[sweep, k], out_send.at[sweep, k], out_recv.at[sweep, k],
            device_id=((row + k) % n_row, col), device_id_type=MESH)

    def to_pair(sweep, k):
        return pltpu.make_async_remote_copy(
            pair_out.at[sweep, k], pair_in.at[sweep, k], pair_send.at[sweep, k], pair_recv.at[sweep, k],
            device_id=(row, chip * 2 + 1 - core), device_id_type=MESH)

    def to_peer(sweep, k):
        return pltpu.make_async_remote_copy(
            mine.at[sweep, k], peer_in.at[sweep, k], peer_send.at[sweep, k], peer_recv.at[sweep, k],
            device_id=(row, ((chip + k) % n_chip) * 2 + core), device_id_type=MESH)

    for k in range(1, n_row):
        to_source(k).start()
    for k in range(1, n_col):
        to_receiver(k).start()
    for k in range(1, n_row):
        to_row(0, k).start()
    source_rows[0] = own_source[...]
    receiver_rows[0] = own_receiver[...]
    for k in range(1, n_row):
        to_source(k).wait_recv()

    sub = lax.broadcasted_iota(I32, (8, block), 0)
    turned[...] = jnp.zeros_like(turned)

    def make_left(k, _):
        owner = (row - k + n_row) % n_row
        for part in range(per_piece):
            h, m, l = pieces(source_rows[k, :, part * block : (part + 1) * block])
            ones = jnp.where(sub < 3, 1.0, 0.0)
            rows = jnp.concatenate([h, h, m, h, l, m, ones, jnp.zeros((72, block), F32)], axis=0)
            turned[...] = rows.T
            for bit in range(8):
                lhs[owner * per_piece + part, bit * words : (bit + 1) * words, :] = (
                    turned[pl.ds(bit, words, stride=8), :].astype(BF16)[:, :64])
        return 0

    lax.fori_loop(0, n_row, make_left, 0)

    for k in range(1, n_col):
        to_receiver(k).wait_recv()

    def make_right(k, _):
        owner = (col - k + n_col) % n_col
        for part in range(per_piece):
            x = receiver_rows[k, :, part * block : (part + 1) * block]
            h, m, l = pieces(x)

            def at(v, row_in, row_out):
                return jnp.where(sub == row_out, pltpu.roll(v, (row_out - row_in) % 8, 0), 0.0)

            def alone(row_in):
                return at(h, row_in, 0) + at(m, row_in, 1) + at(l, row_in, 2)

            zero = jnp.zeros((8, block), F32)
            one_at_7, one_at_3 = jnp.where(sub == 7, 1.0, 0.0), jnp.where(sub == 3, 1.0, 0.0)
            cosine = [jnp.where(sub < 3, v, 0.0) for v in (h, m, l)]
            emitted = [jnp.where((sub > 3) & (sub < 7), v, 0.0) for v in (h, m, l)]
            emitted[0] = emitted[0] + one_at_7
            spread = [jnp.where(sub < 3, pltpu.roll(v, 4, 0) * -2.0, 0.0) for v in (h, m, l)]
            spread[0] = spread[0] + one_at_3
            for n, (v, last) in enumerate(((cosine, alone(3)), (emitted, zero), (spread, alone(7)))):
                full = jnp.concatenate([v[0], v[1], v[0], v[2], v[0], v[1], last, zero], axis=0)
                rhs[owner * per_piece + part, :, n * block : (n + 1) * block] = full.astype(BF16)
        return 0

    lax.fori_loop(0, n_col, make_right, 0)

    fetch.wait()

    def make_factors(step, _):
        for u in range(SLOT_STEP):
            s = step * SLOT_STEP + u
            code = ints[0, s]
            g, h = code // n_source, code % n_source
            for first in range(0, block, CHUNK):
                left = lhs[h, first : first + CHUNK, :]
                met, left_by, spread = (
                    jnp.dot(left, rhs[g, :, n * block : (n + 1) * block], preferred_element_type=F32)
                    for n in range(3))
                bits = range(first // words, (first + CHUNK) // words)
                seen = jnp.concatenate([(seen_words[s] & (1 << bit)) != 0 for bit in bits], axis=0)
                squared = spread * spread
                inverse = pltpu.reciprocal(squared, approx=True)
                inverse = inverse * (2.0 - squared * inverse)
                value = jnp.maximum(met, 0.0) * jnp.maximum(left_by, 0.0) * inverse
                value = jnp.where(seen, value, 0.0)
                high = value.astype(BF16)
                factor_hi[s, first : first + CHUNK, :] = high
                factor_lo[s, first : first + CHUNK, :] = (value - high.astype(F32)).astype(BF16)
        return 0

    lax.fori_loop(0, slots // SLOT_STEP, make_factors, 0)

    for sweep in range(ITERS):
        gathered[sweep, 0] = own_sent[sweep]
        for k in range(1, n_row):
            to_row(sweep, k).wait_recv()

        def split(k, _):
            owner = (row - k + n_row) % n_row
            for part in range(per_piece):
                x = gathered[sweep, k, :, part * block : (part + 1) * block]
                high = x.astype(BF16)
                outgoing[owner * per_piece + part, 0:bands, :] = high
                outgoing[owner * per_piece + part, bands : 2 * bands, :] = (x - high.astype(F32)).astype(BF16)
            return 0

        lax.fori_loop(0, n_row, split, 0)

        def add_slots(step, total):
            for u in range(SWEEP_STEP):
                i = step * SWEEP_STEP + u
                s, h = ints[1, i], ints[2, i]
                left = outgoing[h]
                both = jnp.dot(left, factor_hi[s], preferred_element_type=F32)
                fine = jnp.dot(left[:bands], factor_lo[s], preferred_element_type=F32)
                total = total * floats[0, i] + (both[:bands] + (both[bands:] + fine))
                running[i] = total
            return total

        lax.fori_loop(0, slots // SWEEP_STEP, add_slots, jnp.zeros((bands, block), F32))

        def summed(owner, part):
            g = owner * per_piece + part
            return running[ints[3, g]] * floats[1, g]

        for k in range(n_chip):
            owner = ((chip + k + 1) % n_chip) * 2 + 1 - core
            for part in range(per_piece):
                pair_out[sweep, (k + 1) % n_chip, :, part * block : (part + 1) * block] = summed(owner, part)
            to_pair(sweep, (k + 1) % n_chip).start()
        for k in range(n_chip):
            kk = (k + 1) % n_chip
            owner = ((chip + kk) % n_chip) * 2 + core
            to_pair(sweep, kk).wait_recv()
            for part in range(per_piece):
                lanes = slice(part * block, (part + 1) * block)
                mine[sweep, kk, :, lanes] = summed(owner, part) + pair_in[sweep, kk, :, lanes]
            if kk:
                to_peer(sweep, kk).start()
        total = mine[sweep, 0]
        for k in range(1, n_chip):
            to_peer(sweep, k).wait_recv()
            total = total + peer_in[sweep, k]
        radiosity = emission[...] + reflect[...] * total
        if sweep < ITERS - 1:
            set_sent(sweep + 1, radiosity)
            for k in range(1, n_row):
                to_row(sweep + 1, k).start()
        else:
            out[...] = radiosity

    for k in range(1, n_row):
        to_source(k).wait_send()
    for k in range(1, n_col):
        to_receiver(k).wait_send()
    for sweep in range(ITERS):
        for k in range(1, n_row):
            to_row(sweep, k).wait_send()
        for k in range(n_chip):
            to_pair(sweep, k).wait_send()
        for k in range(1, n_chip):
            to_peer(sweep, k).wait_send()


def slot_order(pair_list, pair_count, n_source, n_receiver):
    codes = pair_list.reshape(-1)
    slots = codes.shape[0]
    slot = jnp.arange(slots, dtype=I32)
    key = jnp.where(slot < pair_count.reshape(()), codes, n_source * n_receiver + slot)
    rank = jnp.sum((key[None, :] < key[:, None]).astype(I32), axis=1)
    hit = rank[None, :] == slot[:, None]
    order = jnp.sum(jnp.where(hit, slot[None, :], 0), axis=1)
    ranked = jnp.sum(jnp.where(hit, key[None, :], 0), axis=1)
    receiver = ranked // n_source
    before = jnp.concatenate([jnp.full((1,), -1, I32), receiver[:-1]])
    block = jnp.arange(slots, dtype=I32)[:, None]
    last = jnp.sum((receiver[None, :] <= block).astype(I32), axis=1) - 1
    any_slot = jnp.any(receiver[None, :] == block, axis=1)
    ints = jnp.stack([codes, order, ranked % n_source, jnp.maximum(last, 0)])
    floats = jnp.stack([(receiver == before).astype(F32), any_slot.astype(F32)])
    return ints, floats


def solution(mesh):
    n_row, n_col = mesh.shape["row"], mesh.shape["col"]

    def body(position, normal, area, emission, reflect, pair_list, pair_count, visible):
        slots, words, block = visible.shape[-3:]
        bands, piece = emission.shape
        per_piece = piece // block
        n_chip = n_col // 2
        n_source, n_receiver = per_piece * n_row, per_piece * n_col
        ints, floats = slot_order(pair_list, pair_count, n_source, n_receiver)
        in_smem = pl.BlockSpec(memory_space=pltpu.SMEM)
        in_vmem = pl.BlockSpec(memory_space=pltpu.VMEM)
        dma = pltpu.SemaphoreType.DMA
        return pl.pallas_call(
            functools.partial(kernel, n_row, n_col),
            out_shape=jax.ShapeDtypeStruct((bands, piece), F32),
            in_specs=[in_smem] * 2 + [in_vmem] * 5 + [pl.BlockSpec(memory_space=pl.ANY)],
            out_specs=in_vmem,
            scratch_shapes=[
                pltpu.VMEM((slots, block, block), BF16),
                pltpu.VMEM((slots, block, block), BF16),
                pltpu.VMEM((slots, words, block), I32),
                pltpu.VMEM((slots, bands, block), F32),
                pltpu.VMEM((n_source, block, 64), BF16),
                pltpu.VMEM((n_receiver, 64, 3 * block), BF16),
                pltpu.VMEM((block, block), BF16),
                pltpu.VMEM((block, 128), F32),
                pltpu.VMEM((8, piece), F32),
                pltpu.VMEM((8, piece), F32),
                pltpu.VMEM((ITERS, bands, piece), F32),
                pltpu.VMEM((n_row, 8, piece), F32),
                pltpu.VMEM((n_col, 8, piece), F32),
                pltpu.VMEM((ITERS, n_row, bands, piece), F32),
                pltpu.VMEM((n_source, 2 * bands, block), BF16),
                pltpu.VMEM((ITERS, n_chip, bands, piece), F32),
                pltpu.VMEM((ITERS, n_chip, bands, piece), F32),
                pltpu.VMEM((ITERS, n_chip, bands, piece), F32),
                pltpu.VMEM((ITERS, n_chip, bands, piece), F32),
                dma,
                dma((n_row,)), dma((n_row,)),
                dma((n_col,)), dma((n_col,)),
                dma((ITERS, n_row)), dma((ITERS, n_row)),
                dma((ITERS, n_chip)), dma((ITERS, n_chip)),
                dma((ITERS, n_chip)), dma((ITERS, n_chip)),
            ],
            compiler_params=pltpu.CompilerParams(
                collective_id=0, has_side_effects=True, vmem_limit_bytes=62 * 2**20),
        )(ints, floats, position, normal, area.reshape(1, piece), emission, reflect,
          visible.reshape(slots, words, block))

    placed = (
        P(None, ("row", "col")),
        P(None, ("row", "col")),
        P(("row", "col")),
        P(None, ("row", "col")),
        P(None, ("row", "col")),
        P("row", "col", None),
        P("row", "col"),
        P("row", "col", None, None, None),
    )
    return jax.shard_map(
        body, mesh=mesh, in_specs=placed, out_specs=P(None, ("row", "col")), check_vma=False
    )
```

time: 1350 us -> 121 us (0.09)
  waiting for transfers between devices: 381 us -> 0 us
  local copies, waits for them, and re-layouts: 292 us -> 1.48 us
  blocking collectives: 215 us -> 0 us
  loops' own time: 178 us -> 0 us
  other arithmetic: 165 us -> 3.06 us
  Pallas kernels: 0 us -> 116 us
  matrix products: 95.8 us -> 0 us
    psum x3 -> x0, waiting for transfers between devices: 381 us -> none  [body(): summed = lax.psum(partial_sum, 'col')]
    all_gather x8 -> x0, blocking collectives: 215 us -> none  [the longest x3 87.7 us: body(): outgoing = lax.all_gather(radiosity, 'row', axis=1, tiled=True)]
    another operation x1 -> x0, loops' own time: 178 us -> none  [body(): factors = lax.map(build_tile, (receiver_ids, source_ids, packed_all))]
    dynamic_slice x512 -> x0, local copies, waits for them, and re-layouts: 169 us -> none  [the longest x256 166 us: body(): factors = lax.map(build_tile, (receiver_ids, source_ids, packed_all))]
    pallas_call x0 -> x1, Pallas kernels: none -> 116 us  [body(): pl.pallas_call(functools.partial(kernel, n_row, n_col), out_shape=jax.Sha...]
    dynamic_update_slice x128 -> x0, other arithmetic: 115 us -> none  [body(): factors = lax.map(build_tile, (receiver_ids, source_ids, packed_all))]
    shift_right_arithmetic x384 -> x0, local copies, waits for them, and re-layouts: 109 us -> none  [tile_factor(): jnp.right_shift(packed_bits[:, None, :], shifts[None, :, None])]
    dot_general x6 -> x0, matrix products: 95.8 us -> none  [the longest x3 75 us: body(): jnp.einsum('bsa,sak->sbk', source_slices, factors, precision=lax.Precisio...]
  transfers between devices with their start and end apart: 3 -> 0, of which waited for: 3 -> 0; matrix products, arithmetic and copies ran while one was open for 0% -> 0% of each run, Pallas kernels for 0% -> 0%
where the time goes in v1:
time: 121 us
  Pallas kernels  116 us (96%)
  other arithmetic  3.06 us (3%)
  local copies, waits for them, and re-layouts  1.48 us (1%)
    pallas_call x1, Pallas kernels, body(): pl.pallas_call(functools.partial(kernel, n_row, n_col), out_shape=jax.Sha...  116 us

profile of v1, /device:TPU:1, one launch (start us, length us, event | category | flops | bytes accessed | tf_op | source)
XLA Modules:
  0.0 121.1 jit_solution(7878949151248707040)
XLA Ops:
  0.7 0.7 compare_select_fusion
  1.3 0.2 convert_reduce_fusion.1
  1.5 0.1 select_reduce_fusion.1
  1.6 0.1 fusion
  1.8 0.1 convert_reduce_fusion
  1.9 0.1 add_compare_fusion
  2.0 0.6 add_convert_fusion.floats
  2.5 1.2 %pad_add_fusion.ints = s32[4,128]{1,0:T(4,128)} fusion(s32[1,128]{1,0:T(1,128)S(1)} %maximum_bitcast_fusion, s32[1,128]{1,0:T(1,128)S(1)} %and_select_fusion.2, s32[1,128]{1,0:T(1,128)S(1)} %bitcast.32, s32[1,128]{1,0:T(1,128)} %bitcast.34), kind=kLoop, calls=%fused_computation.8 | loop fusion | flops 1536 | bytes 4096 | tf_op jit(solution)/shard_map/stack | solution.py:274
  3.8 115.9 %shard_map.82 = f32[32,512]{1,0:T(8,128)} custom-call(s32[4,128]{1,0:T(4,128)} %pad_add_fusion.ints, f32[2,128]{1,0:T(2,128)} %add_convert_fusion.floats, f32[3,512]{1,0:T(4,128)} %position.1, f32[3,512]{1,0:T(4,128)} %normal.1, f32[1,512]{1,0:T(1,128)} %bitcast.31, f32[32,512]{1,0:T(8,128)} %emission.1, f32[32,512]{1,0:T(8,128)} %reflect.1, ...), custom_call_target="tpu_custom_call" | custom-call | tf_op jit(solution)/shard_map/pallas_call | solution.py:292
  119.7 1.5 %copy.11 = f32[32,512]{1,0:T(8,128)} copy(f32[32,512]{1,0:T(8,128)} %shard_map.82) | data formatting | bytes 131072
  (4 shorter events, 0.0 us)

commit v2 on v1

v2 whole, which is shorter than its diff:
```python
import functools
import math

import jax
import jax.numpy as jnp
from jax import lax
from jax.experimental import pallas as pl
from jax.experimental.pallas import tpu as pltpu
from jax.sharding import PartitionSpec as P

ITERS = 3
MESH = pl.DeviceIdType.MESH
F32, BF16, I32 = jnp.float32, jnp.bfloat16, jnp.int32
CHUNK = 64
SLOT_STEP = 16
SWEEP_STEP = 8
PARTS = 2


def pieces(x):
    high = x.astype(BF16).astype(F32)
    rest = x - high
    middle = rest.astype(BF16).astype(F32)
    return high, middle, rest - middle


def kernel(
    n_row, n_col, pair_count, pair_list, position_in, normal_in, area_in, emission_in, reflect_in, visible, out,
    factor_hi, factor_lo, seen_words, running, lhs, rhs, shuffle, turned, own_source, own_receiver,
    own_sent, source_rows, receiver_rows, gathered, outgoing, pair_out, pair_in, mine, peer_in,
    position, normal, area, emission, reflect, codes, table, ints,
    local_sem, table_sem, src_send, src_recv, rec_send, rec_recv, out_send, out_recv, pair_send, pair_recv, peer_send, peer_recv,
):
    slots, words, block = visible.shape
    bands, piece = emission.shape
    per_piece = piece // block
    n_chip = n_col // 2
    n_source, n_receiver = per_piece * n_row, per_piece * n_col
    some = bands // PARTS
    row, col = lax.axis_index("row"), lax.axis_index("col")
    chip, core = col // 2, col % 2

    barrier = pltpu.get_barrier_semaphore()
    for k in range(1, n_row):
        pl.semaphore_signal(barrier, inc=1, device_id=((row + k) % n_row, col), device_id_type=MESH)
    for k in range(1, n_col):
        pl.semaphore_signal(barrier, inc=1, device_id=(row, (col + k) % n_col), device_id_type=MESH)

    fetches = [
        pltpu.make_async_copy(there, here, local_sem.at[n])
        for n, (there, here) in enumerate((
            (position_in, position), (normal_in, normal), (area_in, area), (pair_list, codes),
            (emission_in, emission), (reflect_in, reflect), (visible, seen_words)))
    ]
    for fetch in fetches:
        fetch.start()

    here = lax.broadcasted_iota(I32, (block, block), 0)
    there = lax.broadcasted_iota(I32, (block, block), 1)
    shuffle[...] = jnp.where(here == (there % words) * 8 + there // words, 1.0, 0.0).astype(BF16)

    for fetch in fetches[:3]:
        fetch.wait()

    centre = position[...] - 0.5
    facing = normal[...]
    weight = area[...] * (1.0 / math.pi)
    along = jnp.sum(facing * centre, axis=0, keepdims=True)
    square = jnp.sum(centre * centre, axis=0, keepdims=True)
    own_source[0:3, :] = centre
    own_source[3:4, :] = square + weight
    own_source[4:7, :] = facing * weight
    own_source[7:8, :] = -along * weight
    own_receiver[0:3, :] = facing
    own_receiver[3:4, :] = -along
    own_receiver[4:7, :] = centre
    own_receiver[7:8, :] = square

    def shuffled(x):
        count = x.shape[0]
        cuts = []
        for part in range(per_piece):
            stacked = jnp.concatenate([v.astype(BF16) for v in pieces(x[:, part * block : (part + 1) * block])], axis=0)
            moved = jnp.dot(stacked, shuffle[...], preferred_element_type=F32)
            cuts.append(moved[:count] + moved[count : 2 * count] + moved[2 * count :])
        return jnp.concatenate(cuts, axis=1)

    def lot(q):
        return slice(q * some, (q + 1) * some)

    pl.semaphore_wait(barrier, n_row + n_col - 2)

    def to_source(k):
        return pltpu.make_async_remote_copy(
            own_source, source_rows.at[k], src_send.at[k], src_recv.at[k],
            device_id=((row + k) % n_row, col), device_id_type=MESH)

    def to_receiver(k):
        return pltpu.make_async_remote_copy(
            own_receiver, receiver_rows.at[k], rec_send.at[k], rec_recv.at[k],
            device_id=(row, (col + k) % n_col), device_id_type=MESH)

    def to_row(sweep, q, k):
        return pltpu.make_async_remote_copy(
            own_sent.at[sweep, q], gathered.at[sweep, q, k], out_send.at[sweep, q, k], out_recv.at[sweep, q, k],
            device_id=((row + k) % n_row, col), device_id_type=MESH)

    def to_pair(sweep, q, k):
        return pltpu.make_async_remote_copy(
            pair_out.at[sweep, q, k], pair_in.at[sweep, q, k], pair_send.at[sweep, q, k], pair_recv.at[sweep, q, k],
            device_id=(row, chip * 2 + 1 - core), device_id_type=MESH)

    def to_peer(sweep, q, k):
        return pltpu.make_async_remote_copy(
            mine.at[sweep, q, k], peer_in.at[sweep, q, k], peer_send.at[sweep, q, k], peer_recv.at[sweep, q, k],
            device_id=(row, ((chip + k) % n_chip) * 2 + core), device_id_type=MESH)

    for k in range(1, n_row):
        to_source(k).start()
    for k in range(1, n_col):
        to_receiver(k).start()
    source_rows[0] = own_source[...]
    receiver_rows[0] = own_receiver[...]

    fetches[3].wait()
    below = lax.broadcasted_iota(I32, (slots, slots), 0)
    across = lax.broadcasted_iota(I32, (slots, slots), 1)
    code = codes[...]
    lane = lax.broadcasted_iota(I32, (1, slots), 1)
    key = jnp.where(lane < pair_count[0, 0], code, n_source * n_receiver + lane)
    key_across = jnp.broadcast_to(key, (slots, slots))
    key_below = key_across.T
    rank = jnp.sum((key_below < key_across).astype(I32), axis=0, keepdims=True)
    hit = jnp.broadcast_to(rank, (slots, slots)).T == across
    ranked = jnp.sum(jnp.where(hit, key_below, 0), axis=0, keepdims=True)
    receiver = ranked // n_source
    before = jnp.where(lane == 0, -1, pltpu.roll(receiver, 1, 1))
    table[0:1, :] = code
    table[1:2, :] = jnp.sum(jnp.where(hit, below, 0), axis=0, keepdims=True)
    table[2:3, :] = ranked % n_source
    table[3:4, :] = (receiver == before).astype(I32)
    upto = jnp.sum((key_below // n_source <= across).astype(I32), axis=0, keepdims=True)
    table[4:5, :] = jnp.maximum(upto - 1, 0)
    table[5:6, :] = (jnp.sum((key_below // n_source == across).astype(I32), axis=0, keepdims=True) > 0).astype(I32)
    table[6:8, :] = jnp.zeros((2, slots), I32)
    listing = pltpu.make_async_copy(table, ints, table_sem)
    listing.start()

    fetches[4].wait()
    for q in range(PARTS):
        own_sent[0, q] = shuffled(emission[lot(q), :])
    for k in range(1, n_row):
        to_source(k).wait_recv()

    sub = lax.broadcasted_iota(I32, (8, block), 0)
    turned[...] = jnp.zeros_like(turned)

    def make_left(k, _):
        owner = (row - k + n_row) % n_row
        for part in range(per_piece):
            h, m, l = pieces(source_rows[k, :, part * block : (part + 1) * block])
            ones = jnp.where(sub < 3, 1.0, 0.0)
            rows = jnp.concatenate([h, h, m, h, l, m, ones, jnp.zeros((72, block), F32)], axis=0)
            turned[...] = rows.T
            for bit in range(8):
                lhs[owner * per_piece + part, bit * words : (bit + 1) * words, :] = (
                    turned[pl.ds(bit, words, stride=8), :].astype(BF16)[:, :64])
        return 0

    lax.fori_loop(0, n_row, make_left, 0)

    for k in range(1, n_col):
        to_receiver(k).wait_recv()

    def make_right(k, _):
        owner = (col - k + n_col) % n_col
        for part in range(per_piece):
            x = receiver_rows[k, :, part * block : (part + 1) * block]
            h, m, l = pieces(x)

            def at(v, row_in, row_out):
                return jnp.where(sub == row_out, pltpu.roll(v, (row_out - row_in) % 8, 0), 0.0)

            def alone(row_in):
                return at(h, row_in, 0) + at(m, row_in, 1) + at(l, row_in, 2)

            zero = jnp.zeros((8, block), F32)
            one_at_7, one_at_3 = jnp.where(sub == 7, 1.0, 0.0), jnp.where(sub == 3, 1.0, 0.0)
            cosine = [jnp.where(sub < 3, v, 0.0) for v in (h, m, l)]
            emitted = [jnp.where((sub > 3) & (sub < 7), v, 0.0) for v in (h, m, l)]
            emitted[0] = emitted[0] + one_at_7
            spread = [jnp.where(sub < 3, pltpu.roll(v, 4, 0) * -2.0, 0.0) for v in (h, m, l)]
            spread[0] = spread[0] + one_at_3
            for n, (v, last) in enumerate(((cosine, alone(3)), (emitted, zero), (spread, alone(7)))):
                full = jnp.concatenate([v[0], v[1], v[0], v[2], v[0], v[1], last, zero], axis=0)
                rhs[owner * per_piece + part, :, n * block : (n + 1) * block] = full.astype(BF16)
        return 0

    lax.fori_loop(0, n_col, make_right, 0)

    for q in range(PARTS):
        for k in range(1, n_row):
            to_row(0, q, k).start()
    fetches[5].wait()
    fetches[6].wait()
    listing.wait()

    def make_factors(step, _):
        for u in range(SLOT_STEP):
            s = step * SLOT_STEP + u
            code = ints[0, s]
            g, h = code // n_source, code % n_source
            for first in range(0, block, CHUNK):
                left = lhs[h, first : first + CHUNK, :]
                met, left_by, spread = (
                    jnp.dot(left, rhs[g, :, n * block : (n + 1) * block], preferred_element_type=F32)
                    for n in range(3))
                bits = range(first // words, (first + CHUNK) // words)
                seen = jnp.concatenate([(seen_words[s] & (1 << bit)) != 0 for bit in bits], axis=0)
                squared = spread * spread
                inverse = pltpu.reciprocal(squared, approx=True)
                inverse = inverse * (2.0 - squared * inverse)
                value = jnp.maximum(met, 0.0) * jnp.maximum(left_by, 0.0) * inverse
                value = jnp.where(seen, value, 0.0)
                high = value.astype(BF16)
                factor_hi[s, first : first + CHUNK, :] = high
                factor_lo[s, first : first + CHUNK, :] = (value - high.astype(F32)).astype(BF16)
        return 0

    lax.fori_loop(0, slots // SLOT_STEP, make_factors, 0)

    for sweep in range(ITERS):
        for q in range(PARTS):
            gathered[sweep, q, 0] = own_sent[sweep, q]
            for k in range(1, n_row):
                to_row(sweep, q, k).wait_recv()

            def split(k, _):
                owner = (row - k + n_row) % n_row
                for part in range(per_piece):
                    x = gathered[sweep, q, k, :, part * block : (part + 1) * block]
                    high = x.astype(BF16)
                    at = owner * per_piece + part
                    outgoing[at, q * some : (q + 1) * some, :] = high
                    outgoing[at, bands + q * some : bands + (q + 1) * some, :] = (x - high.astype(F32)).astype(BF16)
                return 0

            lax.fori_loop(0, n_row, split, 0)

        def add_slots(step, total):
            for u in range(SWEEP_STEP):
                i = step * SWEEP_STEP + u
                s, h = ints[1, i], ints[2, i]
                left = outgoing[h]
                both = jnp.dot(left, factor_hi[s], preferred_element_type=F32)
                fine = jnp.dot(left[:bands], factor_lo[s], preferred_element_type=F32)
                total = total * ints[3, i].astype(F32) + (both[:bands] + (both[bands:] + fine))
                running[i] = total
            return total

        lax.fori_loop(0, slots // SWEEP_STEP, add_slots, jnp.zeros((bands, block), F32))

        def summed(owner, part, q):
            g = owner * per_piece + part
            return running[ints[4, g], q * some : (q + 1) * some, :] * ints[5, g].astype(F32)

        order = [k % n_chip for k in range(1, n_chip + 1)]
        for q in range(PARTS):
            for k in order:
                owner = ((chip + k) % n_chip) * 2 + 1 - core
                for part in range(per_piece):
                    pair_out[sweep, q, k, :, part * block : (part + 1) * block] = summed(owner, part, q)
                to_pair(sweep, q, k).start()
        for q in range(PARTS):
            for k in order:
                owner = ((chip + k) % n_chip) * 2 + core
                to_pair(sweep, q, k).wait_recv()
                for part in range(per_piece):
                    lanes = slice(part * block, (part + 1) * block)
                    mine[sweep, q, k, :, lanes] = summed(owner, part, q) + pair_in[sweep, q, k, :, lanes]
                if k:
                    to_peer(sweep, q, k).start()
        for q in range(PARTS):
            total = mine[sweep, q, 0]
            for k in range(1, n_chip):
                to_peer(sweep, q, k).wait_recv()
                total = total + peer_in[sweep, q, k]
            if sweep < ITERS - 1:
                own_sent[sweep + 1, q] = shuffled(emission[lot(q), :] + reflect[lot(q), :] * total)
                for k in range(1, n_row):
                    to_row(sweep + 1, q, k).start()
            else:
                out[lot(q), :] = total

    for k in range(1, n_row):
        to_source(k).wait_send()
    for k in range(1, n_col):
        to_receiver(k).wait_send()
    for sweep in range(ITERS):
        for q in range(PARTS):
            for k in range(1, n_row):
                to_row(sweep, q, k).wait_send()
            for k in range(n_chip):
                to_pair(sweep, q, k).wait_send()
            for k in range(1, n_chip):
                to_peer(sweep, q, k).wait_send()


def solution(mesh):
    n_row, n_col = mesh.shape["row"], mesh.shape["col"]

    def body(position, normal, area, emission, reflect, pair_list, pair_count, visible):
        slots, words, block = visible.shape[-3:]
        bands, piece = emission.shape
        per_piece = piece // block
        n_chip = n_col // 2
        n_source, n_receiver = per_piece * n_row, per_piece * n_col
        in_smem = pl.BlockSpec(memory_space=pltpu.SMEM)
        in_vmem = pl.BlockSpec(memory_space=pltpu.VMEM)
        dma = pltpu.SemaphoreType.DMA
        anywhere = pl.BlockSpec(memory_space=pl.ANY)
        some = bands // PARTS
        gathered = pl.pallas_call(
            functools.partial(kernel, n_row, n_col),
            out_shape=jax.ShapeDtypeStruct((bands, piece), F32),
            in_specs=[in_smem] + [anywhere] * 7,
            out_specs=in_vmem,
            scratch_shapes=[
                pltpu.VMEM((slots, block, block), BF16),
                pltpu.VMEM((slots, block, block), BF16),
                pltpu.VMEM((slots, words, block), I32),
                pltpu.VMEM((slots, bands, block), F32),
                pltpu.VMEM((n_source, block, 64), BF16),
                pltpu.VMEM((n_receiver, 64, 3 * block), BF16),
                pltpu.VMEM((block, block), BF16),
                pltpu.VMEM((block, 128), F32),
                pltpu.VMEM((8, piece), F32),
                pltpu.VMEM((8, piece), F32),
                pltpu.VMEM((ITERS, PARTS, some, piece), F32),
                pltpu.VMEM((n_row, 8, piece), F32),
                pltpu.VMEM((n_col, 8, piece), F32),
                pltpu.VMEM((ITERS, PARTS, n_row, some, piece), F32),
                pltpu.VMEM((n_source, 2 * bands, block), BF16),
                pltpu.VMEM((ITERS, PARTS, n_chip, some, piece), F32),
                pltpu.VMEM((ITERS, PARTS, n_chip, some, piece), F32),
                pltpu.VMEM((ITERS, PARTS, n_chip, some, piece), F32),
                pltpu.VMEM((ITERS, PARTS, n_chip, some, piece), F32),
                pltpu.VMEM((3, piece), F32),
                pltpu.VMEM((3, piece), F32),
                pltpu.VMEM((1, piece), F32),
                pltpu.VMEM((bands, piece), F32),
                pltpu.VMEM((bands, piece), F32),
                pltpu.VMEM((1, slots), I32),
                pltpu.VMEM((8, slots), I32),
                pltpu.SMEM((8, slots), I32),
                dma((7,)),
                dma,
                dma((n_row,)), dma((n_row,)),
                dma((n_col,)), dma((n_col,)),
                dma((ITERS, PARTS, n_row)), dma((ITERS, PARTS, n_row)),
                dma((ITERS, PARTS, n_chip)), dma((ITERS, PARTS, n_chip)),
                dma((ITERS, PARTS, n_chip)), dma((ITERS, PARTS, n_chip)),
            ],
            compiler_params=pltpu.CompilerParams(
                collective_id=0, has_side_effects=True, vmem_limit_bytes=62 * 2**20),
        )(pair_count, pair_list.reshape(1, slots), position, normal, area.reshape(1, piece), emission, reflect,
          visible.reshape(slots, words, block))
        return emission + reflect * gathered

    placed = (
        P(None, ("row", "col")),
        P(None, ("row", "col")),
        P(("row", "col")),
        P(None, ("row", "col")),
        P(None, ("row", "col")),
        P("row", "col", None),
        P("row", "col"),
        P("row", "col", None, None, None),
    )
    return jax.shard_map(
        body, mesh=mesh, in_specs=placed, out_specs=P(None, ("row", "col")), check_vma=False
    )
```

time: 121 us -> 108 us (0.89)
  Pallas kernels: 116 us -> 105 us
  other arithmetic: 3.06 us -> 1.48 us
  local copies, waits for them, and re-layouts: 1.48 us -> 0.01 us
    pallas_call x1, Pallas kernels: 116 us -> 105 us  [body(): pl.pallas_call(functools.partial(kernel, n_row, n_col), out_shape=jax.Sha...]
    another operation x2 -> x0, other arithmetic: 1.79 us -> none  [the longest x1 1.24 us: slot_order(): ints = jnp.stack([codes, order, ranked % n_source, jnp.maximum(last, 0)])]
    add x0 -> x1, other arithmetic: none -> 1.48 us  [body(): return emission + reflect * gathered]
    unnamed x1 -> x4, local copies, waits for them, and re-layouts: 1.47 us -> 0.01 us
where the time goes in v2:
time: 108 us; the launch traced here: 107 us
  Pallas kernels  105 us (97%)
  other arithmetic  1.48 us (1%)
    pallas_call x1, Pallas kernels, body(): pl.pallas_call(functools.partial(kernel, n_row, n_col), out_shape=jax.Sha...  105 us

profile of v2, /device:TPU:1, one launch (start us, length us, event | category | flops | bytes accessed | tf_op | source)
XLA Modules:
  0.0 107.4 jit_solution(13883278530811170493)
XLA Ops:
  0.0 0.0 copy-start.1
  0.0 0.0 copy-start
  0.7 105.2 %shard_map.82 = f32[32,512]{1,0:T(8,128)} custom-call(s32[1,1]{1,0:T(1,128)S(6)} %copy.9.pair_count, s32[1,128]{1,0:T(1,128)} %bitcast.5, f32[3,512]{1,0:T(4,128)} %position_in.1, f32[3,512]{1,0:T(4,128)} %normal_in.1, f32[1,512]{1,0:T(1,128)} %bitcast.4, f32[32,512]{1,0:T(8,128)} %emission_in.1, f32[32,512]{1,0:T(8,128)} %reflect_in.1, s32[128,32,256]{2,1,0:T(8,128)} %bitcast.3), custom_call_target="tpu_custom_call" | custom-call | tf_op jit(solution)/shard_map/pallas_call | solution.py:323
  105.9 0.0 copy-done.1
  105.9 0.0 copy-done
  105.9 1.5 %multiply_add_fusion = f32[32,512]{1,0:T(8,128)} fusion(f32[32,512]{1,0:T(8,128)S(1)} %copy-done, f32[32,512]{1,0:T(8,128)S(1)} %copy-done.1, f32[32,512]{1,0:T(8,128)} %shard_map.82), kind=kLoop, calls=%fused_computation | loop fusion | flops 32768 | bytes 262144 | tf_op jit(solution)/shard_map/add | solution.py:368
Async XLA Ops:
  0.0 105.9 %copy-start.1 = (f32[32,512]{1,0:T(8,128)S(1)}, f32[32,512]{1,0:T(8,128)}, u32[]{:S(2)}) copy-start(f32[32,512]{1,0:T(8,128)} %reflect_in.1) | copy-start | bytes 196612
  0.0 105.9 %copy-start = (f32[32,512]{1,0:T(8,128)S(1)}, f32[32,512]{1,0:T(8,128)}, u32[]{:S(2)}) copy-start(f32[32,512]{1,0:T(8,128)} %emission_in.1) | copy-start | bytes 196612

commit v3 on v2

--- a/solution.py
+++ b/solution.py
@@ -13,7 +13,8 @@
 F32, BF16, I32 = jnp.float32, jnp.bfloat16, jnp.int32
 CHUNK = 64
 SLOT_STEP = 16
-SWEEP_STEP = 8
+SWEEP_STEP = 16
+CUTS = (2, 6)
 PARTS = 2
 
 
@@ -29,7 +30,7 @@
     factor_hi, factor_lo, seen_words, running, lhs, rhs, shuffle, turned, own_source, own_receiver,
     own_sent, source_rows, receiver_rows, gathered, outgoing, pair_out, pair_in, mine, peer_in,
     position, normal, area, emission, reflect, codes, table, ints,
-    local_sem, table_sem, src_send, src_recv, rec_send, rec_recv, out_send, out_recv, pair_send, pair_recv, peer_send, peer_recv,
+    local_sem, table_sem, geo_send, geo_recv, out_send, out_recv, pair_send, pair_recv, peer_send, peer_recv,
 ):
     slots, words, block = visible.shape
     bands, piece = emission.shape
@@ -39,10 +40,24 @@
     some = bands // PARTS
     row, col = lax.axis_index("row"), lax.axis_index("col")
     chip, core = col // 2, col % 2
+    n_x, n_zl = n_row // 2, 2
+    n_y = n_chip // n_zl
+    row_steps = sorted(((a, b) for a in range(2) for b in range(n_x) if a or b), key=lambda s: -(2 * s[0] + min(s[1], n_x - s[1])))
+    chip_steps = sorted(((a, b) for a in range(n_y) for b in range(n_zl) if a or b), key=lambda s: -(min(s[0], n_y - s[0]) + s[1]))
+
+    def row_at(k):
+        a, b = row_steps[k - 1]
+        return ((row // n_x + a) % 2) * n_x + (row % n_x + b) % n_x
+
+    def chip_at(k):
+        if k == 0:
+            return chip
+        a, b = chip_steps[k - 1]
+        return ((chip // n_zl + a) % n_y) * n_zl + (chip % n_zl + b) % n_zl
 
     barrier = pltpu.get_barrier_semaphore()
     for k in range(1, n_row):
-        pl.semaphore_signal(barrier, inc=1, device_id=((row + k) % n_row, col), device_id_type=MESH)
+        pl.semaphore_signal(barrier, inc=1, device_id=(row_at(k), col), device_id_type=MESH)
     for k in range(1, n_col):
         pl.semaphore_signal(barrier, inc=1, device_id=(row, (col + k) % n_col), device_id_type=MESH)
 
@@ -86,41 +101,53 @@
         return jnp.concatenate(cuts, axis=1)
 
     def lot(q):
-        return slice(q * some, (q + 1) * some)
+        return pl.ds(pl.multiple_of(q * some, some), some)
 
     pl.semaphore_wait(barrier, n_row + n_col - 2)
 
     def to_source(k):
         return pltpu.make_async_remote_copy(
-            own_source, source_rows.at[k], src_send.at[k], src_recv.at[k],
-            device_id=((row + k) % n_row, col), device_id_type=MESH)
+            own_source, source_rows.at[row], geo_send.at[0], geo_recv.at[0],
+            device_id=(row_at(k), col), device_id_type=MESH)
 
     def to_receiver(k):
         return pltpu.make_async_remote_copy(
-            own_receiver, receiver_rows.at[k], rec_send.at[k], rec_recv.at[k],
+            own_receiver, receiver_rows.at[col], geo_send.at[1], geo_recv.at[1],
             device_id=(row, (col + k) % n_col), device_id_type=MESH)
 
-    def to_row(sweep, q, k):
+    def to_row(u, k):
         return pltpu.make_async_remote_copy(
-            own_sent.at[sweep, q], gathered.at[sweep, q, k], out_send.at[sweep, q, k], out_recv.at[sweep, q, k],
-            device_id=((row + k) % n_row, col), device_id_type=MESH)
-
-    def to_pair(sweep, q, k):
+            own_sent.at[u], gathered.at[u, row], out_send.at[u], out_recv.at[u],
+            device_id=(row_at(k), col), device_id_type=MESH)
+
+    def to_pair(u):
         return pltpu.make_async_remote_copy(
-            pair_out.at[sweep, q, k], pair_in.at[sweep, q, k], pair_send.at[sweep, q, k], pair_recv.at[sweep, q, k],
+            pair_out.at[u], pair_in.at[u], pair_send.at[u], pair_recv.at[u],
             device_id=(row, chip * 2 + 1 - core), device_id_type=MESH)
 
-    def to_peer(sweep, q, k):
+    def to_peer(u, k):
         return pltpu.make_async_remote_copy(
-            mine.at[sweep, q, k], peer_in.at[sweep, q, k], peer_send.at[sweep, q, k], peer_recv.at[sweep, q, k],
-            device_id=(row, ((chip + k) % n_chip) * 2 + core), device_id_type=MESH)
+            mine.at[u, k], peer_in.at[u, k], peer_send.at[u], peer_recv.at[u],
+            device_id=(row, chip_at(k) * 2 + core), device_id_type=MESH)
+
+    def wait_all(like, sem):
+        pltpu.make_async_copy(like, like, sem).wait()
+
+    all_source = source_rows.at[pl.ds(0, n_row - 1)]
+    all_receiver = receiver_rows.at[pl.ds(0, n_col - 1)]
+
+    def all_row(u):
+        return gathered.at[u, pl.ds(0, n_row - 1)]
+
+    def all_peer(u):
+        return peer_in.at[u, pl.ds(1, n_chip - 1)]
 
     for k in range(1, n_row):
         to_source(k).start()
     for k in range(1, n_col):
         to_receiver(k).start()
-    source_rows[0] = own_source[...]
-    receiver_rows[0] = own_receiver[...]
+    source_rows[row] = own_source[...]
+    receiver_rows[col] = own_receiver[...]
 
     fetches[3].wait()
     below = lax.broadcasted_iota(I32, (slots, slots), 0)
@@ -148,34 +175,31 @@
 
     fetches[4].wait()
     for q in range(PARTS):
-        own_sent[0, q] = shuffled(emission[lot(q), :])
-    for k in range(1, n_row):
-        to_source(k).wait_recv()
+        own_sent[q] = shuffled(emission[lot(q), :])
+    wait_all(all_source, geo_recv.at[0])
 
     sub = lax.broadcasted_iota(I32, (8, block), 0)
     turned[...] = jnp.zeros_like(turned)
 
-    def make_left(k, _):
-        owner = (row - k + n_row) % n_row
+    def make_left(owner, _):
         for part in range(per_piece):
-            h, m, l = pieces(source_rows[k, :, part * block : (part + 1) * block])
+            h, m, l = pieces(source_rows[owner, :, part * block : (part + 1) * block])
             ones = jnp.where(sub < 3, 1.0, 0.0)
             rows = jnp.concatenate([h, h, m, h, l, m, ones, jnp.zeros((72, block), F32)], axis=0)
             turned[...] = rows.T
             for bit in range(8):
                 lhs[owner * per_piece + part, bit * words : (bit + 1) * words, :] = (
                     turned[pl.ds(bit, words, stride=8), :].astype(BF16)[:, :64])
+
         return 0
 
     lax.fori_loop(0, n_row, make_left, 0)
 
-    for k in range(1, n_col):
-        to_receiver(k).wait_recv()
-
-    def make_right(k, _):
-        owner = (col - k + n_col) % n_col
+    wait_all(all_receiver, geo_recv.at[1])
+
+    def make_right(owner, _):
         for part in range(per_piece):
-            x = receiver_rows[k, :, part * block : (part + 1) * block]
+            x = receiver_rows[owner, :, part * block : (part + 1) * block]
             h, m, l = pieces(x)
 
             def at(v, row_in, row_out):
@@ -200,7 +224,7 @@
 
     for q in range(PARTS):
         for k in range(1, n_row):
-            to_row(0, q, k).start()
+            to_row(q, k).start()
     fetches[5].wait()
     fetches[6].wait()
     listing.wait()
@@ -229,81 +253,109 @@
 
     lax.fori_loop(0, slots // SLOT_STEP, make_factors, 0)
 
-    for sweep in range(ITERS):
-        for q in range(PARTS):
-            gathered[sweep, q, 0] = own_sent[sweep, q]
-            for k in range(1, n_row):
-                to_row(sweep, q, k).wait_recv()
-
-            def split(k, _):
-                owner = (row - k + n_row) % n_row
-                for part in range(per_piece):
-                    x = gathered[sweep, q, k, :, part * block : (part + 1) * block]
-                    high = x.astype(BF16)
-                    at = owner * per_piece + part
-                    outgoing[at, q * some : (q + 1) * some, :] = high
-                    outgoing[at, bands + q * some : bands + (q + 1) * some, :] = (x - high.astype(F32)).astype(BF16)
-                return 0
-
-            lax.fori_loop(0, n_row, split, 0)
-
-        def add_slots(step, total):
-            for u in range(SWEEP_STEP):
-                i = step * SWEEP_STEP + u
+    def receive(u):
+        q = u % PARTS
+        gathered[u, row] = own_sent[u]
+        wait_all(all_row(u), out_recv.at[u])
+
+        def split(owner, _):
+            for part in range(per_piece):
+                x = gathered[u, owner, :, part * block : (part + 1) * block]
+                high = x.astype(BF16)
+                outgoing[q, owner * per_piece + part, 0:some, :] = high
+                outgoing[q, owner * per_piece + part, some : 2 * some, :] = (x - high.astype(F32)).astype(BF16)
+            return 0
+
+        lax.fori_loop(0, n_row, split, 0)
+
+    def add_slots(u, first, last, total):
+        q = u % PARTS
+
+        def step(n, total):
+            for i in range(SWEEP_STEP):
+                i = n * SWEEP_STEP + i
                 s, h = ints[1, i], ints[2, i]
-                left = outgoing[h]
+                left = outgoing[q, h]
                 both = jnp.dot(left, factor_hi[s], preferred_element_type=F32)
-                fine = jnp.dot(left[:bands], factor_lo[s], preferred_element_type=F32)
-                total = total * ints[3, i].astype(F32) + (both[:bands] + (both[bands:] + fine))
-                running[i] = total
+                fine = jnp.dot(left[:some], factor_lo[s], preferred_element_type=F32)
+                total = total * ints[3, i].astype(F32) + (both[:some] + (both[some:] + fine))
+                running[q, i] = total
             return total
 
-        lax.fori_loop(0, slots // SWEEP_STEP, add_slots, jnp.zeros((bands, block), F32))
-
-        def summed(owner, part, q):
-            g = owner * per_piece + part
-            return running[ints[4, g], q * some : (q + 1) * some, :] * ints[5, g].astype(F32)
-
-        order = [k % n_chip for k in range(1, n_chip + 1)]
-        for q in range(PARTS):
-            for k in order:
-                owner = ((chip + k) % n_chip) * 2 + 1 - core
-                for part in range(per_piece):
-                    pair_out[sweep, q, k, :, part * block : (part + 1) * block] = summed(owner, part, q)
-                to_pair(sweep, q, k).start()
-        for q in range(PARTS):
-            for k in order:
-                owner = ((chip + k) % n_chip) * 2 + core
-                to_pair(sweep, q, k).wait_recv()
-                for part in range(per_piece):
-                    lanes = slice(part * block, (part + 1) * block)
-                    mine[sweep, q, k, :, lanes] = summed(owner, part, q) + pair_in[sweep, q, k, :, lanes]
-                if k:
-                    to_peer(sweep, q, k).start()
-        for q in range(PARTS):
-            total = mine[sweep, q, 0]
-            for k in range(1, n_chip):
-                to_peer(sweep, q, k).wait_recv()
-                total = total + peer_in[sweep, q, k]
-            if sweep < ITERS - 1:
-                own_sent[sweep + 1, q] = shuffled(emission[lot(q), :] + reflect[lot(q), :] * total)
-                for k in range(1, n_row):
-                    to_row(sweep + 1, q, k).start()
-            else:
-                out[lot(q), :] = total
-
-    for k in range(1, n_row):
-        to_source(k).wait_send()
-    for k in range(1, n_col):
-        to_receiver(k).wait_send()
-    for sweep in range(ITERS):
-        for q in range(PARTS):
-            for k in range(1, n_row):
-                to_row(sweep, q, k).wait_send()
-            for k in range(n_chip):
-                to_pair(sweep, q, k).wait_send()
-            for k in range(1, n_chip):
-                to_peer(sweep, q, k).wait_send()
+        return lax.fori_loop(first, last, step, total)
+
+    def summed(q, owner, part):
+        g = owner * per_piece + part
+        return running[q, ints[4, g]] * ints[5, g].astype(F32)
+
+    order = [k % n_chip for k in range(1, n_chip + 1)]
+
+    def send_pair(u):
+        for k in order:
+            owner = chip_at(k) * 2 + 1 - core
+            for part in range(per_piece):
+                pair_out[u, k, :, part * block : (part + 1) * block] = summed(u % PARTS, owner, part)
+        to_pair(u).start()
+
+    def send_peers(u):
+        to_pair(u).wait_recv()
+        for k in order:
+            owner = chip_at(k) * 2 + core
+            for part in range(per_piece):
+                lanes = slice(part * block, (part + 1) * block)
+                mine[u, k, :, lanes] = summed(u % PARTS, owner, part) + pair_in[u, k, :, lanes]
+            if k:
+                to_peer(u, k).start()
+
+    def gather(u):
+        wait_all(all_peer(u), peer_recv.at[u])
+        total = mine[u, 0]
+        for k in range(1, n_chip):
+            total = total + peer_in[u, k]
+        return total
+
+    def pass_on(u):
+        q = u % PARTS
+        own_sent[u + PARTS] = shuffled(emission[lot(q), :] + reflect[lot(q), :] * gather(u))
+        for k in range(1, n_row):
+            to_row(u + PARTS, k).start()
+
+    steps = slots // SWEEP_STEP
+    halves = PARTS * ITERS
+    nothing = jnp.zeros((some, block), F32)
+    receive(0)
+    add_slots(0, 0, steps, nothing)
+    send_pair(0)
+
+    def half(u, _):
+        send_peers(u - 1)
+        receive(u)
+        cut = jnp.where(u % PARTS == 0, CUTS[0], CUTS[1])
+        total = add_slots(u, 0, cut, nothing)
+        pass_on(u - 1)
+        add_slots(u, cut, steps, total)
+        send_pair(u)
+        return 0
+
+    lax.fori_loop(1, halves - 1, half, 0)
+    send_peers(halves - 2)
+    receive(halves - 1)
+    add_slots(halves - 1, 0, steps, nothing)
+    send_pair(halves - 1)
+    out[lot((halves - 2) % PARTS), :] = gather(halves - 2)
+    send_peers(halves - 1)
+    out[lot((halves - 1) % PARTS), :] = gather(halves - 1)
+
+    wait_all(all_source, geo_send.at[0])
+    wait_all(all_receiver, geo_send.at[1])
+
+    def drain(u, _):
+        wait_all(all_row(u), out_send.at[u])
+        to_pair(u).wait_send()
+        wait_all(all_peer(u), peer_send.at[u])
+        return 0
+
+    lax.fori_loop(0, halves, drain, 0)
 
 
 def solution(mesh):
@@ -329,22 +381,22 @@
                 pltpu.VMEM((slots, block, block), BF16),
                 pltpu.VMEM((slots, block, block), BF16),
                 pltpu.VMEM((slots, words, block), I32),
-                pltpu.VMEM((slots, bands, block), F32),
+                pltpu.VMEM((PARTS, slots, some, block), F32),
                 pltpu.VMEM((n_source, block, 64), BF16),
                 pltpu.VMEM((n_receiver, 64, 3 * block), BF16),
                 pltpu.VMEM((block, block), BF16),
                 pltpu.VMEM((block, 128), F32),
                 pltpu.VMEM((8, piece), F32),
                 pltpu.VMEM((8, piece), F32),
-                pltpu.VMEM((ITERS, PARTS, some, piece), F32),
+                pltpu.VMEM((ITERS * PARTS, some, piece), F32),
                 pltpu.VMEM((n_row, 8, piece), F32),
                 pltpu.VMEM((n_col, 8, piece), F32),
-                pltpu.VMEM((ITERS, PARTS, n_row, some, piece), F32),
-                pltpu.VMEM((n_source, 2 * bands, block), BF16),
-                pltpu.VMEM((ITERS, PARTS, n_chip, some, piece), F32),
-                pltpu.VMEM((ITERS, PARTS, n_chip, some, piece), F32),
-                pltpu.VMEM((ITERS, PARTS, n_chip, some, piece), F32),
-                pltpu.VMEM((ITERS, PARTS, n_chip, some, piece), F32),
+                pltpu.VMEM((ITERS * PARTS, n_row, some, piece), F32),
+                pltpu.VMEM((PARTS, n_source, 2 * some, block), BF16),
+                pltpu.VMEM((ITERS * PARTS, n_chip, some, piece), F32),
+                pltpu.VMEM((ITERS * PARTS, n_chip, some, piece), F32),
+                pltpu.VMEM((ITERS * PARTS, n_chip, some, piece), F32),
+                pltpu.VMEM((ITERS * PARTS, n_chip, some, piece), F32),
                 pltpu.VMEM((3, piece), F32),
                 pltpu.VMEM((3, piece), F32),
                 pltpu.VMEM((1, piece), F32),
@@ -355,11 +407,10 @@
                 pltpu.SMEM((8, slots), I32),
                 dma((7,)),
                 dma,
-                dma((n_row,)), dma((n_row,)),
-                dma((n_col,)), dma((n_col,)),
-                dma((ITERS, PARTS, n_row)), dma((ITERS, PARTS, n_row)),
-                dma((ITERS, PARTS, n_chip)), dma((ITERS, PARTS, n_chip)),
-                dma((ITERS, PARTS, n_chip)), dma((ITERS, PARTS, n_chip)),
+                dma((2,)), dma((2,)),
+                dma((ITERS * PARTS,)), dma((ITERS * PARTS,)),
+                dma((ITERS * PARTS,)), dma((ITERS * PARTS,)),
+                dma((ITERS * PARTS,)), dma((ITERS * PARTS,)),
             ],
             compiler_params=pltpu.CompilerParams(
                 collective_id=0, has_side_effects=True, vmem_limit_bytes=62 * 2**20),

time: 108 us -> 98.9 us (0.916)
  Pallas kernels: 105 us -> 96.5 us
    pallas_call x1, Pallas kernels: 105 us -> 96.5 us  [body(): pl.pallas_call(functools.partial(kernel, n_row, n_col), out_shape=jax.Sha...]
where the time goes in v3:
time: 98.9 us; the launch traced here: 98.7 us
  Pallas kernels  96.5 us (98%)
  other arithmetic  1.48 us (1%)
    pallas_call x1, Pallas kernels, body(): pl.pallas_call(functools.partial(kernel, n_row, n_col), out_shape=jax.Sha...  96.5 us

profile of v3, /device:TPU:1, one launch (start us, length us, event | category | flops | bytes accessed | tf_op | source)
XLA Modules:
  0.0 98.7 jit_solution(3795345072148914015)
XLA Ops:
  0.0 0.0 copy-start.1
  0.0 0.0 copy-start
  0.7 96.5 %shard_map.82 = f32[32,512]{1,0:T(8,128)} custom-call(s32[1,1]{1,0:T(1,128)S(6)} %copy.9.pair_count, s32[1,128]{1,0:T(1,128)} %bitcast.5, f32[3,512]{1,0:T(4,128)} %position_in.1, f32[3,512]{1,0:T(4,128)} %normal_in.1, f32[1,512]{1,0:T(1,128)} %bitcast.4, f32[32,512]{1,0:T(8,128)} %emission_in.1, f32[32,512]{1,0:T(8,128)} %reflect_in.1, s32[128,32,256]{2,1,0:T(8,128)} %bitcast.3), custom_call_target="tpu_custom_call" | custom-call | tf_op jit(solution)/shard_map/pallas_call | solution.py:375
  97.2 0.0 copy-done.1
  97.2 0.0 copy-done
  97.2 1.5 %multiply_add_fusion = f32[32,512]{1,0:T(8,128)} fusion(f32[32,512]{1,0:T(8,128)S(1)} %copy-done, f32[32,512]{1,0:T(8,128)S(1)} %copy-done.1, f32[32,512]{1,0:T(8,128)} %shard_map.82), kind=kLoop, calls=%fused_computation | loop fusion | flops 32768 | bytes 262144 | tf_op jit(solution)/shard_map/add | solution.py:419
Async XLA Ops:
  0.0 97.2 %copy-start.1 = (f32[32,512]{1,0:T(8,128)S(1)}, f32[32,512]{1,0:T(8,128)}, u32[]{:S(2)}) copy-start(f32[32,512]{1,0:T(8,128)} %reflect_in.1) | copy-start | bytes 196612
  0.0 97.2 %copy-start = (f32[32,512]{1,0:T(8,128)S(1)}, f32[32,512]{1,0:T(8,128)}, u32[]{:S(2)}) copy-start(f32[32,512]{1,0:T(8,128)} %emission_in.1) | copy-start | bytes 196612

commit v4 on v3

--- a/solution.py
+++ b/solution.py
@@ -13,8 +13,8 @@
 F32, BF16, I32 = jnp.float32, jnp.bfloat16, jnp.int32
 CHUNK = 64
 SLOT_STEP = 16
-SWEEP_STEP = 16
-CUTS = (2, 6)
+SWEEP_STEP = 32
+CUTS = (1, 3)
 PARTS = 2
 
 
@@ -186,15 +186,18 @@
             h, m, l = pieces(source_rows[owner, :, part * block : (part + 1) * block])
             ones = jnp.where(sub < 3, 1.0, 0.0)
             rows = jnp.concatenate([h, h, m, h, l, m, ones, jnp.zeros((72, block), F32)], axis=0)
-            turned[...] = rows.T
+            turned[part] = rows.T
             for bit in range(8):
                 lhs[owner * per_piece + part, bit * words : (bit + 1) * words, :] = (
-                    turned[pl.ds(bit, words, stride=8), :].astype(BF16)[:, :64])
+                    turned[part, pl.ds(bit, words, stride=8), :].astype(BF16)[:, :64])
 
         return 0
 
-    lax.fori_loop(0, n_row, make_left, 0)
-
+    lax.fori_loop(0, n_row, make_left, 0, unroll=2)
+
+    for q in range(PARTS):
+        for k in range(1, n_row):
+            to_row(q, k).start()
     wait_all(all_receiver, geo_recv.at[1])
 
     def make_right(owner, _):
@@ -220,11 +223,8 @@
                 rhs[owner * per_piece + part, :, n * block : (n + 1) * block] = full.astype(BF16)
         return 0
 
-    lax.fori_loop(0, n_col, make_right, 0)
-
-    for q in range(PARTS):
-        for k in range(1, n_row):
-            to_row(q, k).start()
+    lax.fori_loop(0, n_col, make_right, 0, unroll=4)
+
     fetches[5].wait()
     fetches[6].wait()
     listing.wait()
@@ -243,7 +243,6 @@
                 seen = jnp.concatenate([(seen_words[s] & (1 << bit)) != 0 for bit in bits], axis=0)
                 squared = spread * spread
                 inverse = pltpu.reciprocal(squared, approx=True)
-                inverse = inverse * (2.0 - squared * inverse)
                 value = jnp.maximum(met, 0.0) * jnp.maximum(left_by, 0.0) * inverse
                 value = jnp.where(seen, value, 0.0)
                 high = value.astype(BF16)
@@ -385,7 +384,7 @@
                 pltpu.VMEM((n_source, block, 64), BF16),
                 pltpu.VMEM((n_receiver, 64, 3 * block), BF16),
                 pltpu.VMEM((block, block), BF16),
-                pltpu.VMEM((block, 128), F32),
+                pltpu.VMEM((per_piece, block, 128), F32),
                 pltpu.VMEM((8, piece), F32),
                 pltpu.VMEM((8, piece), F32),
                 pltpu.VMEM((ITERS * PARTS, some, piece), F32),

time: 98.9 us -> 92.2 us (0.932)
  Pallas kernels: 96.5 us -> 89.8 us
    pallas_call x1, Pallas kernels: 96.5 us -> 89.8 us  [body(): pl.pallas_call(functools.partial(kernel, n_row, n_col), out_shape=jax.Sha...]
where the time goes in v4:
time: 92.2 us; the launch traced here: 92 us
  Pallas kernels  89.8 us (97%)
  other arithmetic  1.48 us (2%)
    pallas_call x1, Pallas kernels, body(): pl.pallas_call(functools.partial(kernel, n_row, n_col), out_shape=jax.Sha...  89.8 us

profile of v4, /device:TPU:1, one launch (start us, length us, event | category | flops | bytes accessed | tf_op | source)
XLA Modules:
  0.0 92.0 jit_solution(11435940133725119369)
XLA Ops:
  0.0 0.0 copy-start.1
  0.0 0.0 copy-start
  0.7 89.8 %shard_map.82 = f32[32,512]{1,0:T(8,128)} custom-call(s32[1,1]{1,0:T(1,128)S(6)} %copy.9.pair_count, s32[1,128]{1,0:T(1,128)} %bitcast.5, f32[3,512]{1,0:T(4,128)} %position_in.1, f32[3,512]{1,0:T(4,128)} %normal_in.1, f32[1,512]{1,0:T(1,128)} %bitcast.4, f32[32,512]{1,0:T(8,128)} %emission_in.1, f32[32,512]{1,0:T(8,128)} %reflect_in.1, s32[128,32,256]{2,1,0:T(8,128)} %bitcast.3), custom_call_target="tpu_custom_call" | custom-call | tf_op jit(solution)/shard_map/pallas_call | solution.py:374
  90.5 0.0 copy-done.1
  90.5 0.0 copy-done
  90.5 1.5 %multiply_add_fusion = f32[32,512]{1,0:T(8,128)} fusion(f32[32,512]{1,0:T(8,128)S(1)} %copy-done, f32[32,512]{1,0:T(8,128)S(1)} %copy-done.1, f32[32,512]{1,0:T(8,128)} %shard_map.82), kind=kLoop, calls=%fused_computation | loop fusion | flops 32768 | bytes 262144 | tf_op jit(solution)/shard_map/add | solution.py:418
Async XLA Ops:
  0.0 90.5 %copy-start.1 = (f32[32,512]{1,0:T(8,128)S(1)}, f32[32,512]{1,0:T(8,128)}, u32[]{:S(2)}) copy-start(f32[32,512]{1,0:T(8,128)} %reflect_in.1) | copy-start | bytes 196612
  0.0 90.5 %copy-start = (f32[32,512]{1,0:T(8,128)S(1)}, f32[32,512]{1,0:T(8,128)}, u32[]{:S(2)}) copy-start(f32[32,512]{1,0:T(8,128)} %emission_in.1) | copy-start | bytes 196612

commit v5 on v4

--- a/solution.py
+++ b/solution.py
@@ -120,9 +120,10 @@
             own_sent.at[u], gathered.at[u, row], out_send.at[u], out_recv.at[u],
             device_id=(row_at(k), col), device_id_type=MESH)
 
-    def to_pair(u):
+    def to_pair(u, lot):
+        first = pl.ds(lot * (n_chip // 2), n_chip // 2)
         return pltpu.make_async_remote_copy(
-            pair_out.at[u], pair_in.at[u], pair_send.at[u], pair_recv.at[u],
+            pair_out.at[u, first], pair_in.at[u, first], pair_send.at[u, lot], pair_recv.at[u, lot],
             device_id=(row, chip * 2 + 1 - core), device_id_type=MESH)
 
     def to_peer(u, k):
@@ -265,7 +266,7 @@
                 outgoing[q, owner * per_piece + part, some : 2 * some, :] = (x - high.astype(F32)).astype(BF16)
             return 0
 
-        lax.fori_loop(0, n_row, split, 0)
+        lax.fori_loop(0, n_row, split, 0, unroll=True)
 
     def add_slots(u, first, last, total):
         q = u % PARTS
@@ -293,16 +294,20 @@
         for k in order:
             owner = chip_at(k) * 2 + 1 - core
             for part in range(per_piece):
-                pair_out[u, k, :, part * block : (part + 1) * block] = summed(u % PARTS, owner, part)
-        to_pair(u).start()
+                pair_out[u, (k - 1) % n_chip, :, part * block : (part + 1) * block] = summed(u % PARTS, owner, part)
+            if k == n_chip // 2:
+                to_pair(u, 0).start()
+        to_pair(u, 1).start()
 
     def send_peers(u):
-        to_pair(u).wait_recv()
+        to_pair(u, 0).wait_recv()
         for k in order:
+            if k == n_chip // 2 + 1:
+                to_pair(u, 1).wait_recv()
             owner = chip_at(k) * 2 + core
             for part in range(per_piece):
                 lanes = slice(part * block, (part + 1) * block)
-                mine[u, k, :, lanes] = summed(u % PARTS, owner, part) + pair_in[u, k, :, lanes]
+                mine[u, k, :, lanes] = summed(u % PARTS, owner, part) + pair_in[u, (k - 1) % n_chip, :, lanes]
             if k:
                 to_peer(u, k).start()
 
@@ -350,7 +355,8 @@
 
     def drain(u, _):
         wait_all(all_row(u), out_send.at[u])
-        to_pair(u).wait_send()
+        to_pair(u, 0).wait_send()
+        to_pair(u, 1).wait_send()
         wait_all(all_peer(u), peer_send.at[u])
         return 0
 
@@ -408,7 +414,7 @@
                 dma,
                 dma((2,)), dma((2,)),
                 dma((ITERS * PARTS,)), dma((ITERS * PARTS,)),
-                dma((ITERS * PARTS,)), dma((ITERS * PARTS,)),
+                dma((ITERS * PARTS, 2)), dma((ITERS * PARTS, 2)),
                 dma((ITERS * PARTS,)), dma((ITERS * PARTS,)),
             ],
             compiler_params=pltpu.CompilerParams(

time: 92.2 us -> 91.2 us (0.989)
    pallas_call x1, Pallas kernels: 89.8 us -> 88.9 us  [body(): pl.pallas_call(functools.partial(kernel, n_row, n_col), out_shape=jax.Sha...]
where the time goes in v5:
time: 91.2 us; the launch traced here: 91.1 us
  Pallas kernels  88.9 us (97%)
  other arithmetic  1.48 us (2%)
    pallas_call x1, Pallas kernels, body(): pl.pallas_call(functools.partial(kernel, n_row, n_col), out_shape=jax.Sha...  88.9 us

profile of v5, /device:TPU:1, one launch (start us, length us, event | category | flops | bytes accessed | tf_op | source)
XLA Modules:
  0.0 91.1 jit_solution(3999338344993463806)
XLA Ops:
  0.0 0.0 copy-start.1
  0.0 0.0 copy-start
  0.7 88.9 %shard_map.82 = f32[32,512]{1,0:T(8,128)} custom-call(s32[1,1]{1,0:T(1,128)S(6)} %copy.9.pair_count, s32[1,128]{1,0:T(1,128)} %bitcast.5, f32[3,512]{1,0:T(4,128)} %position_in.1, f32[3,512]{1,0:T(4,128)} %normal_in.1, f32[1,512]{1,0:T(1,128)} %bitcast.4, f32[32,512]{1,0:T(8,128)} %emission_in.1, f32[32,512]{1,0:T(8,128)} %reflect_in.1, s32[128,32,256]{2,1,0:T(8,128)} %bitcast.3), custom_call_target="tpu_custom_call" | custom-call | tf_op jit(solution)/shard_map/pallas_call | solution.py:380
  89.6 0.0 copy-done.1
  89.6 0.0 copy-done
  89.6 1.5 %multiply_add_fusion = f32[32,512]{1,0:T(8,128)} fusion(f32[32,512]{1,0:T(8,128)S(1)} %copy-done, f32[32,512]{1,0:T(8,128)S(1)} %copy-done.1, f32[32,512]{1,0:T(8,128)} %shard_map.82), kind=kLoop, calls=%fused_computation | loop fusion | flops 32768 | bytes 262144 | tf_op jit(solution)/shard_map/add | solution.py:424
Async XLA Ops:
  0.0 89.6 %copy-start.1 = (f32[32,512]{1,0:T(8,128)S(1)}, f32[32,512]{1,0:T(8,128)}, u32[]{:S(2)}) copy-start(f32[32,512]{1,0:T(8,128)} %reflect_in.1) | copy-start | bytes 196612
  0.0 89.6 %copy-start = (f32[32,512]{1,0:T(8,128)S(1)}, f32[32,512]{1,0:T(8,128)}, u32[]{:S(2)}) copy-start(f32[32,512]{1,0:T(8,128)} %emission_in.1) | copy-start | bytes 196612

commit v6 on v5

--- a/solution.py
+++ b/solution.py
@@ -110,10 +110,10 @@
             own_source, source_rows.at[row], geo_send.at[0], geo_recv.at[0],
             device_id=(row_at(k), col), device_id_type=MESH)
 
-    def to_receiver(k):
+    def to_receiver(k, other):
         return pltpu.make_async_remote_copy(
             own_receiver, receiver_rows.at[col], geo_send.at[1], geo_recv.at[1],
-            device_id=(row, (col + k) % n_col), device_id_type=MESH)
+            device_id=(row, chip_at(k) * 2 + (core + other) % 2), device_id_type=MESH)
 
     def to_row(u, k):
         return pltpu.make_async_remote_copy(
@@ -143,10 +143,12 @@
     def all_peer(u):
         return peer_in.at[u, pl.ds(1, n_chip - 1)]
 
+    for k in range(1, n_chip):
+        for other in range(2):
+            to_receiver(k, other).start()
     for k in range(1, n_row):
         to_source(k).start()
-    for k in range(1, n_col):
-        to_receiver(k).start()
+    to_receiver(0, 1).start()
     source_rows[row] = own_source[...]
     receiver_rows[col] = own_receiver[...]
 

time: 91.2 us -> 91.9 us (level)
  no operation moved by 1% of the time
where the time goes in v6:
time: 91.9 us; the launch traced here: 91.7 us
  Pallas kernels  89.5 us (97%)
  other arithmetic  1.48 us (2%)
    pallas_call x1, Pallas kernels, body(): pl.pallas_call(functools.partial(kernel, n_row, n_col), out_shape=jax.Sha...  89.5 us

profile of v6, /device:TPU:1, one launch (start us, length us, event | category | flops | bytes accessed | tf_op | source)
XLA Modules:
  0.0 91.7 jit_solution(7314978879105352608)
XLA Ops:
  0.0 0.0 copy-start.1
  0.0 0.0 copy-start
  0.7 89.5 %shard_map.82 = f32[32,512]{1,0:T(8,128)} custom-call(s32[1,1]{1,0:T(1,128)S(6)} %copy.9.pair_count, s32[1,128]{1,0:T(1,128)} %bitcast.5, f32[3,512]{1,0:T(4,128)} %position_in.1, f32[3,512]{1,0:T(4,128)} %normal_in.1, f32[1,512]{1,0:T(1,128)} %bitcast.4, f32[32,512]{1,0:T(8,128)} %emission_in.1, f32[32,512]{1,0:T(8,128)} %reflect_in.1, s32[128,32,256]{2,1,0:T(8,128)} %bitcast.3), custom_call_target="tpu_custom_call" | custom-call | tf_op jit(solution)/shard_map/pallas_call | solution.py:382
  90.2 0.0 copy-done.1
  90.2 0.0 copy-done
  90.2 1.5 %multiply_add_fusion = f32[32,512]{1,0:T(8,128)} fusion(f32[32,512]{1,0:T(8,128)S(1)} %copy-done, f32[32,512]{1,0:T(8,128)S(1)} %copy-done.1, f32[32,512]{1,0:T(8,128)} %shard_map.82), kind=kLoop, calls=%fused_computation | loop fusion | flops 32768 | bytes 262144 | tf_op jit(solution)/shard_map/add | solution.py:426
Async XLA Ops:
  0.0 90.2 %copy-start.1 = (f32[32,512]{1,0:T(8,128)S(1)}, f32[32,512]{1,0:T(8,128)}, u32[]{:S(2)}) copy-start(f32[32,512]{1,0:T(8,128)} %reflect_in.1) | copy-start | bytes 196612
  0.0 90.2 %copy-start = (f32[32,512]{1,0:T(8,128)S(1)}, f32[32,512]{1,0:T(8,128)}, u32[]{:S(2)}) copy-start(f32[32,512]{1,0:T(8,128)} %emission_in.1) | copy-start | bytes 196612
